TPU v7x, 1024 devices: a whole 4x8x16 slice. The times are simulated.
1024 devices in a mesh: dp: 128 (over y, z), fsdp: 8 (over x, core).
Axes of the slice: x: 4, y: 8, z: 16, core: 2. Of those that a mesh axis runs over, the one named last changes fastest.
Arguments:
- crops: bfloat16 [1024, 4, 8, 8, 256], P(('dp', 'fsdp')), may hold values from -6 to 6
- weight: bfloat16 [256, 27, 128], P('fsdp'), may hold values from -0.078125 to 0.078125
- bucket_bias: float32 [8, 128], replicated, may hold values from -4 to 4
- norm_gain: float32 [128], replicated, may hold values from 0.25 to 1.75
- norm_shift: float32 [128], replicated, may hold values from -3 to 3
- bucket_ids: int32 [1024], P(('dp', 'fsdp')), may hold values from 0 to 7
- valid_counts: int32 [1024], P(('dp', 'fsdp')), may hold values from 64 to 256
- cotangent: bfloat16 [1024, 256, 128], P(('dp', 'fsdp')), may hold values from -0.011962891 to 0.011962891
Outputs:
- activated: bfloat16 [1024, 256, 128], P(('dp', 'fsdp'))
- weight_grad: float32 [256, 27, 128], P('fsdp')
All inputs are finite; a program needn't handle non-finite values.
Results may differ from a plain program's by a relative error of at most 0.0029.
Values may be sent and summed in bfloat16 or wider, within the bound.
A program may use at most 32 MiB of HBM per device.

v0:
```python
import jax
import jax.numpy as jnp
from jax import lax
from jax.sharding import PartitionSpec as P

GSIZE = 8


epsilon = 1e-05


def normalize(pre_norm, mask_col, count, gain, shift, bias_row):
    voxels, chans = pre_norm.shape
    grouped = pre_norm.reshape(voxels, chans // GSIZE, GSIZE)
    weights = mask_col[:, :, None]
    entries = count.astype(jnp.float32) * GSIZE
    mean_val = jnp.sum(grouped * weights, axis=(0, 2)) / entries
    centered = grouped - mean_val[None, :, None]
    var_val = jnp.sum(centered * centered * weights, axis=(0, 2)) / entries
    normed = (centered * lax.rsqrt(var_val + epsilon)[None, :, None]).reshape(voxels, chans)
    return jax.nn.silu(normed * gain + shift + bias_row) * mask_col


def build_columns(padded, count):
    depth_cells = padded.shape[0] - 2
    row_cells = padded.shape[1] - 2
    col_cells = padded.shape[2] - 2
    voxels = depth_cells * row_cells * col_cells
    slabs = []
    for tap_index in range(27):
        depth_off = tap_index // 9
        row_off = tap_index // 3 % 3
        col_off = tap_index % 3
        slab = padded[
            depth_off : depth_off + depth_cells,
            row_off : row_off + row_cells,
            col_off : col_off + col_cells,
            :,
        ]
        slabs.append(slab.reshape(voxels, count))
    return jnp.stack(slabs, axis=-1).reshape(voxels, count * 27)


def pad_volume(masked):
    return jnp.pad(masked, ((1, 1), (1, 1), (1, 1), (0, 0)))


def body(crops, weight, bucket_bias, norm_gain, norm_shift, bucket_ids, valid_counts, cotangent):
    volume = crops[0]
    count = valid_counts[0]
    bucket = bucket_ids[0]
    depth_cells, row_cells, col_cells, in_chans = volume.shape
    voxels = depth_cells * row_cells * col_cells
    taps_count = weight.shape[1]
    out_chans = weight.shape[2]
    own_rows = weight.shape[0]
    mask_col = (lax.iota(jnp.int32, voxels) < count).astype(jnp.float32)[:, None]
    masked = (
        volume.astype(jnp.float32) * mask_col.reshape(depth_cells, row_cells, col_cells, 1)
    ).astype(jnp.bfloat16)
    padded = pad_volume(masked)
    piece = lax.all_gather(weight, "fsdp", axis=0, tiled=True)
    rows_here = piece.shape[0]
    columns = build_columns(padded, rows_here)
    pre_norm = jnp.dot(
        columns,
        piece.reshape(rows_here * taps_count, out_chans),
        preferred_element_type=jnp.float32,
    )
    bias_row = jnp.sum(
        jnp.where(lax.iota(jnp.int32, bucket_bias.shape[0])[:, None] == bucket, bucket_bias, 0.0),
        axis=0,
    )
    outputs, pullback = jax.vjp(
        lambda value: normalize(value, mask_col, count, norm_gain, norm_shift, bias_row), pre_norm
    )
    grad_pre = pullback(cotangent[0].astype(jnp.float32))[0].astype(jnp.bfloat16)
    columns = build_columns(padded, own_rows * lax.axis_size("fsdp"))
    product = lax.dot_general(
        columns, grad_pre, (((0,), (0,)), ((), ())), preferred_element_type=jnp.float32
    )
    shard_sum = lax.psum_scatter(
        product.reshape(own_rows * lax.axis_size("fsdp"), taps_count, out_chans),
        "fsdp",
        scatter_dimension=0,
        tiled=True,
    )
    weight_grad = lax.psum(shard_sum, "dp")
    activated = outputs.astype(jnp.bfloat16)[None]
    return (activated, weight_grad)


def solution(mesh):
    return jax.shard_map(
        body,
        mesh=mesh,
        in_specs=(
            P(("dp", "fsdp"), None, None, None, None),
            P("fsdp", None, None),
            P(),
            P(),
            P(),
            P(("dp", "fsdp")),
            P(("dp", "fsdp")),
            P(("dp", "fsdp"), None, None),
        ),
        out_specs=(P(("dp", "fsdp"), None, None), P("fsdp", None, None)),
        check_vma=False,
    )
```

profile of v0, /device:TPU:28, one launch (start us, length us, event | category | flops | bytes accessed | tf_op | source)
XLA Modules:
  0.0 409.7 jit_solution(5591322835690532063)
XLA Ops:
  8.6 1.0 fusion.6
  9.6 1.5 pad_slice_fusion
  11.1 0.9 pad_slice_fusion.1
  12.3 1.1 constant_dynamic-update-slice_fusion.26
  13.4 0.9 constant_dynamic-update-slice_fusion.25
  14.3 0.9 constant_dynamic-update-slice_fusion.24
  15.2 0.9 constant_dynamic-update-slice_fusion.23
  16.1 0.9 constant_dynamic-update-slice_fusion.22
  17.0 0.9 constant_dynamic-update-slice_fusion.21
  18.0 0.9 constant_dynamic-update-slice_fusion.20
  18.9 0.9 constant_dynamic-update-slice_fusion.19
  19.8 0.9 constant_dynamic-update-slice_fusion.18
  20.7 0.9 constant_dynamic-update-slice_fusion.17
  21.6 0.9 constant_dynamic-update-slice_fusion.16
  22.6 0.9 constant_dynamic-update-slice_fusion.15
  23.5 0.9 constant_dynamic-update-slice_fusion.14
  24.4 1.0 constant_dynamic-update-slice_fusion.13
  25.8 6.1 %copy.82 = bf16[256,256,27]{0,2,1:T(8,128)(2,1)} copy(bf16[256,256,27]{1,0,2:T(8,128)(2,1)S(1)} %constant_dynamic-update-slice_fusion) | data formatting | bytes 7077888 | tf_op jit(solution)/shard_map/stack | solution.py:41
  31.9 5.0 %reshape.257 = bf16[256,6912]{0,1:T(8,128)(2,1)S(1)} reshape(bf16[256,256,27]{0,2,1:T(8,128)(2,1)} %copy.82) | data formatting | bytes 7077888 | tf_op jit(solution)/shard_map/reshape | solution.py:41
  38.4 1.6 copy.88
  40.1 0.7 add.89
  41.5 2.9 dot_general.18
  44.4 1.5 bitcast_convert_fusion
  45.9 6.6 %all-gather.2.cloned.1.call-done = bf16[256,27,128]{2,0,1:T(8,128)(2,1)} async-done(((bf16[32,27,128]{2,0,1:T(8,128)(2,1)}), bf16[256,27,128]{2,0,1:T(8,128)(2,1)}) %all-gather.2.cloned.1.call-update) | async-done | bytes 1769488 | tf_op jit(solution)/shard_map/all_gather | solution.py:62
  52.5 4.0 copy.83
  56.5 3.9 reshape.258
  60.4 3.9 copy.84
  64.3 2.4 multiply_reduce_fusion.2
  67.5 5.7 %fusion.2 = f32[256,27,128]{2,0,1:T(8,128)} fusion(bf16[256,27,256]{2,1,0:T(8,128)(2,1)S(1)} %copy-done, bf16[256,16,8]{0,1,2:T(8,128)(2,1)S(1)} %add_convert_fusion), kind=kOutput, calls=%fused_computation.28 | convolution fusion | flops 452984832 | bytes 7143424 | tf_op jit(solution)/shard_map/dot_general | solution.py:79
  73.3 44.0 %reduce-scatter.2.cloned.1.call-done = f32[32,27,128]{2,0,1:T(8,128)} async-done(((f32[256,27,128]{2,0,1:T(8,128)}), f32[32,27,128]{2,0,1:T(8,128)}) %reduce-scatter.2.cloned.1.call-update) | async-done | bytes 442384 | tf_op jit(solution)/shard_map/reduce_scatter | solution.py:82
  118.2 283.1 %all-reduce.3.cloned.1.call-done = f32[32,27,128]{2,0,1:T(8,128)} async-done(((f32[32,27,128]{2,0,1:T(8,128)}), f32[32,27,128]{2,0,1:T(8,128)}) %all-reduce.3.cloned.1.call-update) | async-done | bytes 442384 | tf_op jit(solution)/shard_map/psum | solution.py:88
  401.4 1.8 copy.147
  (83 shorter events, 4.5 us)
Async XLA Ops:
  7.2 45.3 %all-gather.2.cloned.1.call-start = ((), (), s32[]{:S(2)}) async-start(), calls=%async_computation.1 | async-start | bytes 1990656 | tf_op jit(solution)/shard_map/all_gather | solution.py:62
  7.9 109.4 %reduce-scatter.2.cloned.1.call-start = ((), (), s32[]{:S(2)}) async-start(), calls=%async_computation.2 | async-start | bytes 3981312 | tf_op jit(solution)/shard_map/reduce_scatter | solution.py:82
  12.2 13.2 %copy-start.7 = (bf16[4,8,8,256]{3,2,1,0:T(8,128)(2,1)S(1)}, bf16[4,8,8,256]{3,2,1,0:T(8,128)(2,1)}, u32[]{:S(2)}) copy-start(bf16[4,8,8,256]{3,2,1,0:T(8,128)(2,1)} %get-tuple-element.26) | copy-start | bytes 393220
  12.2 13.3 %copy-start.6 = (bf16[4,8,8,256]{3,2,1,0:T(8,128)(2,1)S(1)}, bf16[4,8,8,256]{3,2,1,0:T(8,128)(2,1)}, u32[]{:S(2)}) copy-start(bf16[4,8,8,256]{3,2,1,0:T(8,128)(2,1)} %get-tuple-element.27) | copy-start | bytes 393220
  12.2 13.3 %copy-start.5 = (bf16[4,8,8,256]{3,2,1,0:T(8,128)(2,1)S(1)}, bf16[4,8,8,256]{3,2,1,0:T(8,128)(2,1)}, u32[]{:S(2)}) copy-start(bf16[4,8,8,256]{3,2,1,0:T(8,128)(2,1)} %get-tuple-element.28) | copy-start | bytes 393220
  12.2 13.3 %copy-start.4 = (bf16[4,8,8,256]{3,2,1,0:T(8,128)(2,1)S(1)}, bf16[4,8,8,256]{3,2,1,0:T(8,128)(2,1)}, u32[]{:S(2)}) copy-start(bf16[4,8,8,256]{3,2,1,0:T(8,128)(2,1)} %get-tuple-element.29) | copy-start | bytes 393220
  12.2 13.3 %copy-start.3 = (bf16[4,8,8,256]{3,2,1,0:T(8,128)(2,1)S(1)}, bf16[4,8,8,256]{3,2,1,0:T(8,128)(2,1)}, u32[]{:S(2)}) copy-start(bf16[4,8,8,256]{3,2,1,0:T(8,128)(2,1)} %get-tuple-element.30) | copy-start | bytes 393220
  12.2 13.3 %copy-start.2 = (bf16[4,8,8,256]{3,2,1,0:T(8,128)(2,1)S(1)}, bf16[4,8,8,256]{3,2,1,0:T(8,128)(2,1)}, u32[]{:S(2)}) copy-start(bf16[4,8,8,256]{3,2,1,0:T(8,128)(2,1)} %get-tuple-element.31) | copy-start | bytes 393220
  12.2 13.3 %copy-start.14 = (bf16[4,8,8,256]{3,2,1,0:T(8,128)(2,1)S(1)}, bf16[4,8,8,256]{3,2,1,0:T(8,128)(2,1)}, u32[]{:S(2)}) copy-start(bf16[4,8,8,256]{3,2,1,0:T(8,128)(2,1)} %get-tuple-element.33) | copy-start | bytes 393220
  12.2 13.4 %copy-start.13 = (bf16[4,8,8,256]{3,2,1,0:T(8,128)(2,1)S(1)}, bf16[4,8,8,256]{3,2,1,0:T(8,128)(2,1)}, u32[]{:S(2)}) copy-start(bf16[4,8,8,256]{3,2,1,0:T(8,128)(2,1)} %get-tuple-element.34) | copy-start | bytes 393220
  12.3 13.4 %copy-start.12 = (bf16[4,8,8,256]{3,2,1,0:T(8,128)(2,1)S(1)}, bf16[4,8,8,256]{3,2,1,0:T(8,128)(2,1)}, u32[]{:S(2)}) copy-start(bf16[4,8,8,256]{3,2,1,0:T(8,128)(2,1)} %get-tuple-element.35) | copy-start | bytes 393220
  12.3 13.4 %copy-start.11 = (bf16[4,8,8,256]{3,2,1,0:T(8,128)(2,1)S(1)}, bf16[4,8,8,256]{3,2,1,0:T(8,128)(2,1)}, u32[]{:S(2)}) copy-start(bf16[4,8,8,256]{3,2,1,0:T(8,128)(2,1)} %get-tuple-element.36) | copy-start | bytes 393220
  12.3 13.4 %copy-start.10 = (bf16[4,8,8,256]{3,2,1,0:T(8,128)(2,1)S(1)}, bf16[4,8,8,256]{3,2,1,0:T(8,128)(2,1)}, u32[]{:S(2)}) copy-start(bf16[4,8,8,256]{3,2,1,0:T(8,128)(2,1)} %get-tuple-element.37) | copy-start | bytes 393220
  12.3 13.4 %copy-start.9 = (bf16[4,8,8,256]{3,2,1,0:T(8,128)(2,1)S(1)}, bf16[4,8,8,256]{3,2,1,0:T(8,128)(2,1)}, u32[]{:S(2)}) copy-start(bf16[4,8,8,256]{3,2,1,0:T(8,128)(2,1)} %get-tuple-element.32) | copy-start | bytes 393220
  12.3 13.5 %copy-start.1 = (bf16[4,8,8,256]{3,2,1,0:T(8,128)(2,1)S(1)}, bf16[4,8,8,256]{3,2,1,0:T(8,128)(2,1)}, u32[]{:S(2)}) copy-start(bf16[4,8,8,256]{3,2,1,0:T(8,128)(2,1)} %get-tuple-element.13) | copy-start | bytes 393220
  31.9 5.7 %copy-start.18 = (f32[8,128]{1,0:T(8,128)S(1)}, f32[8,128]{1,0:T(8,128)}, u32[]{:S(2)}) copy-start(f32[8,128]{1,0:T(8,128)} %param.10) | copy-start | bytes 12292
  31.9 8.1 %copy-start.20 = (f32[128]{0:T(128)S(1)}, f32[128]{0:T(128)}, u32[]{:S(2)}) copy-start(f32[128]{0:T(128)} %param.11) | copy-start | bytes 1540
  37.6 0.6 copy-start.16
  64.3 2.6 copy-start.8
  64.3 2.6 copy-start.15
  64.3 3.2 copy-start
  73.3 44.1 %copy-start.17 = (f32[128]{0:T(128)S(1)}, f32[128]{0:T(128)}, u32[]{:S(2)}) copy-start(f32[128]{0:T(128)} %copy-done.16) | copy-start | bytes 1540
  73.3 44.1 %copy-start.19 = (f32[128]{0:T(128)S(1)}, f32[128]{0:T(128)}, u32[]{:S(2)}) copy-start(f32[128]{0:T(128)} %param.12) | copy-start | bytes 1540
  73.3 44.1 %copy-start.21 = (f32[128]{0:T(128)S(1)}, f32[128]{0:T(128)}, u32[]{:S(2)}) copy-start(f32[128]{0:T(128)} %param.11) | copy-start | bytes 1540
  73.3 328.1 %all-reduce.3.cloned.1.call-start = ((), (), s32[]{:S(2)}) async-start(), calls=%async_computation.3 | async-start | bytes 884736 | tf_op jit(solution)/shard_map/psum | solution.py:88
Sparse Core Ops, SparseCore 0:
  10.7 41.7 all-gather.1
  73.4 43.8 reduce-scatter.1
  121.2 280.1 all-reduce.2
where the time goes:
time: 411 us; the launch traced here: 410 us
  waiting for transfers between devices  334 us (81%)
  local copies, waits for them, and re-layouts  47 us (11%)
  between operations  15.5 us (4%)
  matrix products  8.09 us (2%)
  other arithmetic  4.6 us (1%)
    psum x1, waiting for transfers between devices, body(): weight_grad = lax.psum(shard_sum, 'dp')  283 us
    reduce_scatter x1, waiting for transfers between devices, body(): lax.psum_scatter(product.reshape(own_rows * lax.axis_size('fsdp'), taps_c...  44 us
    unnamed x72, local copies, waits for them, and re-layouts  17 us
  transfers between devices with their start and end apart: 3, of which 3 were waited for; matrix products, arithmetic and copies ran while one was open for 9% of the time, Pallas kernels for 0%

commit v1 on v0

v1 whole, which is shorter than its diff:
```python
import functools

import jax
import jax.numpy as jnp
from jax import lax
from jax.experimental import pallas as pl
from jax.experimental.pallas import tpu as pltpu
from jax.sharding import PartitionSpec as P

MESH = pl.DeviceIdType.MESH
F32 = jnp.float32
BF16 = jnp.bfloat16

EPSILON = 1e-05
VOX = 256
OWN = 32
OUTS = 128
QUARTER = 32
TAPS = 27
TILES = 7
COLS = TILES * 128
UNITS = 16
REAL = 2 * TILES
CHUNKS = ((0, 256), (256, 256), (512, 256), (768, 128))


def lane_fields():
    lane = lax.broadcasted_iota(jnp.int32, (8, VOX), 1)
    return lane >> 6, (lane >> 3) & 7, lane & 7


def inside(offset, field, cells):
    moved = field + offset
    return jnp.logical_and(moved >= 0, moved < cells)[0:1]


def wait_bytes(ref, sem):
    pltpu.make_async_copy(ref, ref, sem).wait()


def kernel(
    geometry,
    count_ref, bucket_ref, crop_ref, weight_ref, bias_ref, gain_ref, shift_ref, cot_ref,
    act_ref, grad_ref,
    x_ref, xt_ref, wf_ref, wg_ref, wt_ref, ct_ref, c4_ref, meta_ref, par_ref,
    g_ref, dwf_ref, d1s_ref, d1r_ref, s_ref, r2_ref, f_ref, acts_ref, actr_ref,
    w_send, w_recv, x_send, x_recv, c_send, c_recv, m_send, m_recv, a_send, a_recv,
    d1_send, d1_recv, d2_send, d2_recv, e1_send, e1_recv, e2_send, e2_recv,
):
    ny, nz, peers = geometry
    nyp, nzp = ny // 2, nz // 2
    per_row = UNITS // nyp
    per_dev = max(1, per_row // nzp)
    stride = max(1, nzp // per_row)
    chans = OWN * peers

    dp = lax.axis_index("dp")
    fs = lax.axis_index("fsdp")
    y, z = dp // nz, dp % nz
    yp, zp, qy, qz = y // 2, z // 2, y % 2, z % 2
    q = qy * 2 + qz

    def plane(yy, zz):
        return (yy * nz + zz, fs)

    def along(k):
        return (dp, lax.rem(fs + k, peers))

    def member(k):
        return plane(2 * yp + (qy ^ (k >> 1)), 2 * zp + (qz ^ (k & 1)))

    barrier = pltpu.get_barrier_semaphore()

    def greet(device):
        pl.semaphore_signal(barrier, inc=1, device_id=device, device_id_type=MESH)

    for k in range(1, peers):
        greet(along(k))
    for k in range(1, 4):
        greet(member(k))
    greeted = peers - 1 + 3

    @pl.loop(1, nyp * nzp)
    def _(i):
        yy = lax.rem(yp + i // nzp, nyp)
        zz = lax.rem(zp + i % nzp, nzp)
        greet(plane(2 * yy + qy, 2 * zz + qz))

    greeted += nyp * nzp - 1
    for k in range(1, nzp):
        greet(plane(y, 2 * lax.rem(zp + k, nzp) + 1 - qz))
    for k in range(1, nyp):
        greet(plane(2 * lax.rem(yp + k, nyp) + 1 - qy, z))
    greeted += nzp - 1 + nyp - 1

    count = count_ref[0]
    bucket = bucket_ref[0]
    rows = lax.broadcasted_iota(jnp.int32, (VOX, 1), 0)
    row_mask = (rows < count).astype(F32)
    x_ref[0] = (crop_ref[...].astype(F32) * row_mask).astype(BF16)

    for c in range(OWN):
        wf_ref[pl.ds(32 * c, TAPS), :] = weight_ref[c].astype(F32)
    lane_block = lax.broadcasted_iota(jnp.int32, (OWN, 128), 1) >> 5
    mine = pl.ds(pl.multiple_of(OWN * fs, OWN), OWN)
    for g in range(TILES):
        tile = jnp.zeros((OWN, 128), F32)
        for j in range(4):
            if 4 * g + j < TAPS:
                tap = wf_ref[pl.ds(4 * g + j, OWN, stride=32), :]
                tap = pltpu.roll(tap, lax.rem(32 * (j - q) + 128, 128), 1)
                tile = jnp.where(lane_block == j, tap, tile)
        wg_ref[mine, pl.ds(128 * g, 128)] = tile.astype(BF16)

    ct_ref[...] = cot_ref[...].astype(F32).T.astype(BF16)
    bias_rows = lax.broadcasted_iota(jnp.int32, (8, OUTS), 0)
    bias_row = jnp.sum(jnp.where(bias_rows == bucket, bias_ref[...], 0.0), axis=0, keepdims=True)
    meta_ref[0] = jnp.where(bias_rows == 0, bias_row, count.astype(F32))

    pl.semaphore_wait(barrier, greeted)

    w_copies = []
    for k in range(1, peers):
        copy = pltpu.make_async_remote_copy(
            src_ref=wg_ref.at[mine, :], dst_ref=wg_ref.at[mine, :],
            send_sem=w_send.at[k - 1], recv_sem=w_recv, device_id=along(k), device_id_type=MESH,
        )
        copy.start()
        w_copies.append(copy)
    block_copies = []
    for k in range(1, 4):
        to = pl.ds(pl.multiple_of(QUARTER * (q ^ k), QUARTER), QUARTER)
        for src, dst, send, recv in (
            (meta_ref.at[0], meta_ref.at[k], m_send, m_recv),
            (ct_ref.at[to, :], c4_ref.at[k], c_send, c_recv),
            (x_ref.at[0], x_ref.at[k], x_send, x_recv),
        ):
            copy = pltpu.make_async_remote_copy(
                src_ref=src, dst_ref=dst, send_sem=send.at[k - 1], recv_sem=recv.at[k - 1],
                device_id=member(k), device_id_type=MESH,
            )
            copy.start()
            block_copies.append(copy)
    quarter = pl.ds(pl.multiple_of(QUARTER * q, QUARTER), QUARTER)
    c4_ref[0] = ct_ref[quarter, :]

    for k in range(1, 4):
        wait_bytes(meta_ref.at[k], m_recv.at[k - 1])
    table = jnp.concatenate(
        [meta_ref[k, 0:1, :] for k in range(4)]
        + [gain_ref[...], shift_ref[...], jnp.zeros((122, OUTS), F32)],
        axis=0,
    )
    par_ref[...] = table.T
    params = par_ref[quarter, :]
    param_lane = lax.broadcasted_iota(jnp.int32, (QUARTER, OUTS), 1)

    def column(index):
        return jnp.sum(jnp.where(param_lane == index, params, 0.0), axis=1, keepdims=True)

    gain = column(4)
    shift = column(5)

    if peers > 1:
        wait_bytes(wg_ref.at[pl.ds(0, OWN * (peers - 1)), :], w_recv)
    for g in range(TILES):
        wt_ref[pl.ds(128 * g, 128), :] = wg_ref[:, pl.ds(128 * g, 128)].astype(F32).T.astype(BF16)

    zf, yf, xf = lane_fields()
    reach = {
        (axis, offset): inside(offset, field, cells).astype(F32)
        for axis, field, cells in (("z", zf, 4), ("y", yf, 8), ("x", xf, 8))
        for offset in (-1, 1)
    }

    def moved(value, axis, offset, step):
        if offset == 0:
            return value
        rolled = pltpu.roll(value, (-offset * step) % VOX, 1)
        return rolled * reach[axis, offset]

    def group_sum(value):
        grouped = value.reshape(QUARTER // 8, 8, VOX)
        total = jnp.sum(jnp.sum(grouped, axis=2, keepdims=True), axis=1, keepdims=True)
        return total

    def per_crop(m, carry):
        @pl.when(m > 0)
        def _():
            wait_bytes(x_ref.at[m], x_recv.at[m - 1])
            wait_bytes(c4_ref.at[m], c_recv.at[m - 1])

        xt = x_ref[m].astype(F32).T.astype(BF16)
        xt_ref[m] = xt
        pre = jnp.zeros((QUARTER, VOX), F32)
        sum_z = sum_y = None
        for g in range(TILES):
            product = jnp.dot(wt_ref[pl.ds(128 * g, 128), :], xt, preferred_element_type=F32)
            for j in range(4):
                t = 4 * g + j
                if t >= TAPS:
                    continue
                a, b, e = t // 9 - 1, t // 3 % 3 - 1, t % 3 - 1
                part = moved(product[32 * j : 32 * j + 32], "x", e, 1)
                sum_y = part if e == -1 else sum_y + part
                if e == 1:
                    part = moved(sum_y, "y", b, 8)
                    sum_z = part if b == -1 else sum_z + part
                    if b == 1:
                        pre = pre + moved(sum_z, "z", a, 64)

        cells = meta_ref[m][1:2, 0:1]
        lane = lax.broadcasted_iota(jnp.int32, (1, VOX), 1).astype(F32)
        mask = (lane < cells).astype(F32)
        inverse = 1.0 / (cells * 8.0)
        inverse = inverse.reshape(1, 1, 1)

        def spread(total):
            return jnp.broadcast_to(total, (QUARTER // 8, 8, VOX)).reshape(QUARTER, VOX)

        mean = spread(group_sum(pre * mask) * inverse)
        centered = pre - mean
        variance = group_sum(centered * centered * mask) * inverse
        scale = spread(lax.rsqrt(variance + EPSILON))
        normed = centered * scale
        value = normed * gain + shift + column(m)
        sig = 1.0 / (1.0 + jnp.exp(-value))
        acts_ref[m] = (value * sig * mask).astype(BF16)
        d_normed = c4_ref[m].astype(F32) * mask * (sig * (1.0 + value * (1.0 - sig))) * gain
        mean_d = spread(group_sum(d_normed) * inverse)
        mean_dn = spread(group_sum(d_normed * normed) * inverse)
        grad = scale * (d_normed - mask * (mean_d + normed * mean_dn))
        grad = grad.astype(BF16).astype(F32)
        for a in range(-1, 2):
            grad_a = moved(grad, "z", -a, 64)
            for b in range(-1, 2):
                grad_ab = moved(grad_a, "y", -b, 8)
                for e in range(-1, 2):
                    t = 9 * (a + 1) + 3 * (b + 1) + e + 1
                    g_ref[m, pl.ds(32 * t, 32), :] = moved(grad_ab, "x", -e, 1).astype(BF16)
        g_ref[m, pl.ds(32 * TAPS, 32), :] = jnp.zeros((32, VOX), BF16)
        return carry

    lax.fori_loop(0, 4, per_crop, 0)

    act_copies = []
    for k in range(1, 4):
        copy = pltpu.make_async_remote_copy(
            src_ref=acts_ref.at[k], dst_ref=actr_ref.at[quarter, :],
            send_sem=a_send.at[k - 1], recv_sem=a_recv.at[k - 1],
            device_id=member(k), device_id_type=MESH,
        )
        copy.start()
        act_copies.append(copy)
    actr_ref[quarter, :] = acts_ref[0]

    d1_copies = []
    for index, (start, width) in enumerate(CHUNKS):
        lanes = pl.ds(start, width)
        total = jnp.zeros((chans, width), F32)
        for m in range(4):
            total = total + lax.dot_general(
                xt_ref[m], g_ref[m, lanes, :], (((1,), (1,)), ((), ())), preferred_element_type=F32
            )
        dwf_ref[:, lanes] = total
        d1s_ref[:, lanes] = total.astype(BF16)
        for k in range(1, peers):
            theirs = pl.ds(pl.multiple_of(OWN * lax.rem(fs + k, peers), OWN), OWN)
            copy = pltpu.make_async_remote_copy(
                src_ref=d1s_ref.at[theirs, lanes], dst_ref=d1r_ref.at[k - 1, :, lanes],
                send_sem=d1_send.at[index], recv_sem=d1_recv.at[index],
                device_id=along(k), device_id_type=MESH,
            )
            copy.start()
            d1_copies.append(copy)

    def owner(u):
        place = u % per_row
        if per_dev > 1:
            return u // per_row, place // per_dev
        return u // per_row, place * stride

    d2_copies = []
    for index, (start, width) in enumerate(CHUNKS):
        lanes = pl.ds(start, width)
        if peers > 1:
            wait_bytes(d1r_ref.at[:, :, lanes], d1_recv.at[index])
        total = dwf_ref[mine, lanes]
        for k in range(1, peers):
            total = total + d1r_ref[k - 1, :, lanes].astype(F32)
        for g in range(start // 128, (start + width) // 128):
            for h in range(2):
                u = 2 * g + h
                at = 128 * g - start
                s_ref[u] = total[16 * h : 16 * h + 16, at : at + 128]
                oy, oz = owner(u)
                away = jnp.logical_or(yp != oy, zp != oz)
                slot = lax.rem(yp - oy + nyp, nyp) * nzp + lax.rem(zp - oz + nzp, nzp) - 1
                copy = pltpu.make_async_remote_copy(
                    src_ref=s_ref.at[u],
                    dst_ref=r2_ref.at[u % per_dev, jnp.maximum(slot, 0)],
                    send_sem=d2_send.at[u], recv_sem=d2_recv.at[u % per_dev],
                    device_id=plane(2 * oy + qy, 2 * oz + qz), device_id_type=MESH,
                )
                pl.when(away)(copy.start)
                d2_copies.append((away, copy))

    if per_dev > 1:
        owns = yp >= 0
        first = yp * per_row + zp * per_dev
    else:
        owns = lax.rem(zp, stride) == 0
        first = yp * per_row + zp // stride

    def row_peer(k):
        return plane(y, lax.rem(z + k, nz))

    def place_of(u):
        return lax.rem(u, per_row)

    @pl.when(owns)
    def _():
        for i in range(per_dev):
            u = first + i

            @pl.when(u < REAL)
            def _():
                wait_bytes(r2_ref.at[i], d2_recv.at[i])
                total = s_ref[u]
                for k in range(nyp * nzp - 1):
                    total = total + r2_ref[i, k]
                f_ref[u, qy, qz] = total.astype(BF16)

            @pl.when(u >= REAL)
            def _():
                f_ref[u, qy, qz] = jnp.zeros((16, 128), BF16)

            for k in range(1, nz):
                pltpu.make_async_remote_copy(
                    src_ref=f_ref.at[u, qy, qz], dst_ref=f_ref.at[u, qy, qz],
                    send_sem=e1_send.at[i, k - 1], recv_sem=e1_recv.at[place_of(u), qz],
                    device_id=row_peer(k), device_id_type=MESH,
                ).start()

    for k in range(1, 4):
        theirs = pl.ds(pl.multiple_of(QUARTER * (q ^ k), QUARTER), QUARTER)
        wait_bytes(actr_ref.at[theirs, :], a_recv.at[k - 1])
    act_ref[...] = actr_ref[...].astype(F32).T.astype(BF16)

    for place in range(per_row):
        u = yp * per_row + place
        for side in range(2):
            if per_dev > 1:
                local = jnp.logical_and(zp == place // per_dev, qz == side)
            else:
                local = jnp.logical_and(zp == place * stride, qz == side)

            @pl.when(jnp.logical_not(local))
            def _():
                wait_bytes(f_ref.at[u, qy, side], e1_recv.at[place, side])

    row_units = f_ref.at[pl.ds(pl.multiple_of(yp * per_row, per_row), per_row), qy]
    e2_copies = []
    for k in range(1, ny):
        copy = pltpu.make_async_remote_copy(
            src_ref=row_units, dst_ref=row_units,
            send_sem=e2_send.at[k - 1], recv_sem=e2_recv.at[k - 1],
            device_id=plane(lax.rem(y + k, ny), z), device_id_type=MESH,
        )
        copy.start()
        e2_copies.append(copy)
    for copy in e2_copies:
        copy.wait_recv()

    block16 = lax.broadcasted_iota(jnp.int32, (16, 128), 1) >> 5
    for g in range(TILES):
        for h in range(2):
            quarters = [f_ref[2 * g + h, p // 2, p % 2].astype(F32) for p in range(4)]
            for j in range(4):
                t = 4 * g + j
                if t >= TAPS:
                    continue
                line = jnp.zeros((16, 128), F32)
                for p in range(4):
                    turned = quarters[p] if p == j else pltpu.roll(quarters[p], (32 * (p - j)) % 128, 1)
                    line = jnp.where(block16 == p, turned, line)
                grad_ref[pl.ds(16 * h * 32 + t, 16, stride=32), :] = line
    for c in range(OWN):
        grad_ref[pl.ds(32 * c + TAPS, 32 - TAPS), :] = jnp.zeros((32 - TAPS, 128), F32)

    for copy in w_copies + block_copies + act_copies + e2_copies:
        copy.wait_send()
    if peers > 1:
        for index, (start, width) in enumerate(CHUNKS):
            wait_bytes(d1r_ref.at[:, :, pl.ds(start, width)], d1_send.at[index])
    for away, copy in d2_copies:
        pl.when(away)(copy.wait_send)

    @pl.when(owns)
    def _():
        for i in range(per_dev):
            for k in range(1, nz):
                wait_bytes(f_ref.at[first + i, qy, qz], e1_send.at[i, k - 1])


def body(geometry, crops, weight, bucket_bias, norm_gain, norm_shift, bucket_ids, valid_counts, cotangent):
    ny, nz, peers = geometry
    nyp, nzp = ny // 2, nz // 2
    per_row = UNITS // nyp
    per_dev = max(1, per_row // nzp)
    chans = OWN * peers
    others = max(1, peers - 1)
    smem = pl.BlockSpec(memory_space=pltpu.SMEM)
    vmem = pl.BlockSpec(memory_space=pltpu.VMEM)
    dma = pltpu.SemaphoreType.DMA
    activated, grad = pl.pallas_call(
        functools.partial(kernel, geometry),
        out_shape=(
            jax.ShapeDtypeStruct((VOX, OUTS), BF16),
            jax.ShapeDtypeStruct((OWN * 32, OUTS), F32),
        ),
        in_specs=[smem, smem] + [vmem] * 6,
        out_specs=(vmem, vmem),
        scratch_shapes=[
            pltpu.VMEM((4, VOX, chans), BF16),
            pltpu.VMEM((4, chans, VOX), BF16),
            pltpu.VMEM((OWN * 32, OUTS), F32),
            pltpu.VMEM((chans, COLS), BF16),
            pltpu.VMEM((COLS, chans), BF16),
            pltpu.VMEM((OUTS, VOX), BF16),
            pltpu.VMEM((4, QUARTER, VOX), BF16),
            pltpu.VMEM((4, 8, OUTS), F32),
            pltpu.VMEM((OUTS, OUTS), F32),
            pltpu.VMEM((4, COLS, VOX), BF16),
            pltpu.VMEM((chans, COLS), F32),
            pltpu.VMEM((chans, COLS), BF16),
            pltpu.VMEM((others, OWN, COLS), BF16),
            pltpu.VMEM((REAL, 16, 128), F32),
            pltpu.VMEM((per_dev, nyp * nzp - 1, 16, 128), F32),
            pltpu.VMEM((UNITS, 2, 2, 16, 128), BF16),
            pltpu.VMEM((4, QUARTER, VOX), BF16),
            pltpu.VMEM((OUTS, VOX), BF16),
            dma((others,)), dma,
            dma((3,)), dma((3,)),
            dma((3,)), dma((3,)),
            dma((3,)), dma((3,)),
            dma((3,)), dma((3,)),
            dma((len(CHUNKS),)), dma((len(CHUNKS),)),
            dma((REAL,)), dma((per_dev,)),
            dma((per_dev, nz - 1)), dma((per_row, 2)),
            dma((ny - 1,)), dma((ny - 1,)),
        ],
        compiler_params=pltpu.CompilerParams(
            collective_id=0, has_side_effects=True, vmem_limit_bytes=40 * 1024 * 1024
        ),
    )(
        valid_counts, bucket_ids,
        crops.reshape(VOX, chans), weight, bucket_bias,
        norm_gain.reshape(1, OUTS), norm_shift.reshape(1, OUTS), cotangent.reshape(VOX, OUTS),
    )
    weight_grad = grad.reshape(OWN, 32, OUTS)[:, :TAPS, :]
    return activated[None], weight_grad


def solution(mesh):
    chips = mesh.shape["dp"]
    ny = 8 if chips == 128 else 2
    geometry = (ny, chips // ny, mesh.shape["fsdp"])
    return jax.shard_map(
        functools.partial(body, geometry),
        mesh=mesh,
        in_specs=(
            P(("dp", "fsdp"), None, None, None, None),
            P("fsdp", None, None),
            P(),
            P(),
            P(),
            P(("dp", "fsdp")),
            P(("dp", "fsdp")),
            P(("dp", "fsdp"), None, None),
        ),
        out_specs=(P(("dp", "fsdp"), None, None), P("fsdp", None, None)),
        check_vma=False,
    )
```

time: 411 us -> 78.9 us (0.19)
  the two profiles are of different devices: /device:TPU:28 before, /device:TPU:1 now
where the time goes in v1:
time: 78.9 us; the launch traced here: 78.7 us
  Pallas kernels  73.9 us (94%)
  local copies, waits for them, and re-layouts  2.79 us (4%)
  between operations  2.01 us (3%)
    pallas_call x1, Pallas kernels, body(): pl.pallas_call(functools.partial(kernel, geometry), out_shape=(jax.ShapeD...  73.9 us
    unnamed x13, local copies, waits for them, and re-layouts  2.79 us

profile of v1, /device:TPU:1, one launch (start us, length us, event | category | flops | bytes accessed | tf_op | source)
XLA Modules:
  0.0 78.7 jit_solution(17676243643984738944)
XLA Ops:
  1.9 0.0 copy-start
  1.9 0.0 copy-start.1
  1.9 0.0 copy-start.2
  2.0 0.0 copy-start.3
  2.0 0.0 copy-start.4
  2.0 1.1 %copy.10.weight_ref = bf16[32,27,128]{2,1,0:T(8,128)(2,1)S(1)} copy(bf16[32,27,128]{2,0,1:T(8,128)(2,1)} %param.9) | data formatting | bytes 442368 | tf_op args[1]
  3.1 0.0 copy-done
  3.1 0.0 copy-done.1
  3.1 0.0 copy-done.2
  3.1 0.0 copy-done.3
  3.1 0.0 copy-done.4
  3.1 73.9 %shard_map.95 = (bf16[256,128]{1,0:T(8,128)(2,1)S(1)}, f32[1024,128]{1,0:T(8,128)S(1)}) custom-call(s32[1]{0:T(128)S(6)} %copy.15.count_ref, s32[1]{0:T(128)S(6)} %copy.14.bucket_ref, bf16[256,256]{1,0:T(8,128)(2,1)S(1)} %bitcast.8, bf16[32,27,128]{2,1,0:T(8,128)(2,1)S(1)} %copy.10.weight_ref, f32[8,128]{1,0:T(8,128)S(1)} %copy-done.2, ...), custom_call_target="tpu_custom_call" | custom-call | tf_op jit(solution)/shard_map/pallas_call | solution.py:416
  77.0 1.0 %copy.12 = f32[32,27,128]{2,0,1:T(8,128)} copy(f32[32,27,128]{2,1,0:T(8,128)S(1)} %bitcast.7) | data formatting | bytes 884736
  78.1 0.6 copy.16
Async XLA Ops:
  1.9 1.2 %copy-start = (bf16[1,4,8,8,256]{4,3,2,1,0:T(8,128)(2,1)S(1)}, bf16[1,4,8,8,256]{4,3,2,1,0:T(8,128)(2,1)}, u32[]{:S(2)}) copy-start(bf16[1,4,8,8,256]{4,3,2,1,0:T(8,128)(2,1)} %param.8) | copy-start | bytes 393220
  1.9 1.2 %copy-start.1 = (bf16[1,256,128]{2,1,0:T(8,128)(2,1)S(1)}, bf16[1,256,128]{2,1,0:T(8,128)(2,1)}, u32[]{:S(2)}) copy-start(bf16[1,256,128]{2,1,0:T(8,128)(2,1)} %param.15) | copy-start | bytes 196612
  1.9 1.2 %copy-start.2 = (f32[8,128]{1,0:T(8,128)S(1)}, f32[8,128]{1,0:T(8,128)}, u32[]{:S(2)}) copy-start(f32[8,128]{1,0:T(8,128)} %bias_ref.1) | copy-start | bytes 12292
  2.0 1.2 %copy-start.3 = (f32[128]{0:T(128)S(1)}, f32[128]{0:T(128)}, u32[]{:S(2)}) copy-start(f32[128]{0:T(128)} %param.11) | copy-start | bytes 1540
  2.0 1.2 %copy-start.4 = (f32[128]{0:T(128)S(1)}, f32[128]{0:T(128)}, u32[]{:S(2)}) copy-start(f32[128]{0:T(128)} %param.12) | copy-start | bytes 1540

commit v2 on v1

v2 whole, which is shorter than its diff:
```python
import functools

import jax
import jax.numpy as jnp
from jax import lax
from jax.experimental import pallas as pl
from jax.experimental.pallas import tpu as pltpu
from jax.sharding import PartitionSpec as P

MESH = pl.DeviceIdType.MESH
F32 = jnp.float32
BF16 = jnp.bfloat16

EPSILON = 1e-05
VOX = 256
OWN = 32
OUTS = 128
QUARTER = 32
TAPS = 27
TILES = 7
COLS = TILES * 128
UNITS = 16
REAL = 2 * TILES
CHUNKS = ((0, 256), (256, 256), (512, 256), (768, 128))


def lane_fields():
    lane = lax.broadcasted_iota(jnp.int32, (8, VOX), 1)
    return lane >> 6, (lane >> 3) & 7, lane & 7


def inside(offset, field, cells):
    moved = field + offset
    return jnp.logical_and(moved >= 0, moved < cells)[0:1]


def wait_bytes(ref, sem):
    pltpu.make_async_copy(ref, ref, sem).wait()


def kernel(
    geometry,
    count_ref, bucket_ref, crop_hbm, weight_hbm, bias_hbm, gain_hbm, shift_hbm, cot_hbm,
    act_ref, grad_ref,
    crop_ref, weight_ref, bias_ref, gain_ref, shift_ref, cot_ref, in_sem,
    x_ref, xt_ref, wg_ref, wt_ref, ct_ref, c4_ref, meta_ref, par_ref,
    g_ref, dwf_ref, d0r_ref, d1s_ref, d1r_ref, s_ref, r2_ref, f_ref, acts_ref, actr_ref,
    told, w_send, w_recv, x_send, x_recv, c_send, c_recv, m_send, m_recv, a_send, a_recv,
    d0_send, d0_recv, d1_send, d1_recv, d2_send, d2_recv, e1_send, e1_recv, e2_send, e2_recv,
):
    ny, nz, peers = geometry
    nyp, nzp = ny // 2, nz // 2
    per_row = UNITS // nyp
    spots = min(per_row, nzp, 4)
    per_dev = per_row // spots
    chans = OWN * peers

    dp = lax.axis_index("dp")
    fs = lax.axis_index("fsdp")
    y, z = dp // nz, dp % nz
    yp, zp, qy, qz = y // 2, z // 2, y % 2, z % 2
    q = qy * 2 + qz

    def plane(yy, zz):
        return (yy * nz + zz, fs)

    def along(k):
        return (dp, lax.rem(fs + k, peers))

    def member(k):
        return plane(2 * yp + (qy ^ (k >> 1)), 2 * zp + (qz ^ (k & 1)))

    loads = [
        pltpu.make_async_copy(src, dst, in_sem.at[index])
        for index, (src, dst) in enumerate((
            (crop_hbm, crop_ref), (weight_hbm, weight_ref), (cot_hbm, cot_ref),
            (bias_hbm, bias_ref), (gain_hbm, gain_ref), (shift_hbm, shift_ref),
        ))
    ]
    for load in loads:
        load.start()

    barrier = pltpu.get_barrier_semaphore()

    def greet(device):
        pl.semaphore_signal(barrier, inc=1, device_id=device, device_id_type=MESH)

    for k in range(1, peers):
        greet(along(k))
    for k in range(1, 4):
        greet(member(k))
    greeted = peers - 1 + 3

    beside = sorted({(a % nyp, b % nzp) for a in (-1, 0, 1) for b in (-1, 0, 1)} - {(0, 0)})
    beyond = sorted({2 % nzp, -2 % nzp} - {0})

    def block(a, b):
        return plane(2 * lax.rem(yp + a, nyp) + qy, 2 * lax.rem(zp + b, nzp) + qz)

    for a, b in beside:
        greet(block(a, b))
    greeted += len(beside)

    def tell(step, devices):
        for device in devices:
            pl.semaphore_signal(told.at[step], inc=1, device_id=device, device_id_type=MESH)

    def hear(step, devices):
        if devices:
            pl.semaphore_wait(told.at[step], len(devices))

    rounds = (
        [block(a, b) for a, b in beside],
        [block(0, b) for b in beyond],
        [member(k) for k in range(1, 4)],
    )

    count = count_ref[0]
    bucket = bucket_ref[0]
    rows = lax.broadcasted_iota(jnp.int32, (VOX, 1), 0)
    row_mask = (rows < count).astype(F32)
    loads[0].wait()
    x_ref[0] = (crop_ref[...].astype(F32) * row_mask).astype(BF16)

    pl.semaphore_wait(barrier, greeted)
    pending = []

    def send_block(src, dst, send, recv, k):
        copy = pltpu.make_async_remote_copy(
            src_ref=src, dst_ref=dst, send_sem=send.at[k - 1], recv_sem=recv.at[k - 1],
            device_id=member(k), device_id_type=MESH,
        )
        copy.start()
        pending.append(copy.wait_send)

    for k in (3, 1, 2):
        send_block(x_ref.at[0], x_ref.at[k], x_send, x_recv, k)

    lane_block = lax.broadcasted_iota(jnp.int32, (OWN, 128), 1) >> 5
    mine = pl.ds(pl.multiple_of(OWN * fs, OWN), OWN)
    loads[1].wait()
    for g in range(TILES):
        tile = jnp.zeros((OWN, 128), F32)
        for j in range(4):
            if 4 * g + j < TAPS:
                tap = weight_ref[4 * g + j].astype(F32)
                tap = pltpu.roll(tap, lax.rem(32 * (j - q) + 128, 128), 1)
                tile = jnp.where(lane_block == j, tap, tile)
        wg_ref[mine, pl.ds(128 * g, 128)] = tile.astype(BF16)


    chips_x = peers // 2
    sibling = (dp, fs + 1 - 2 * lax.rem(fs, 2))

    def piece(k):
        return pl.ds(pl.multiple_of(OWN * lax.rem(fs + 2 * k, peers), OWN), OWN)

    def send_piece(rows, index, device):
        copy = pltpu.make_async_remote_copy(
            src_ref=wg_ref.at[rows, :], dst_ref=wg_ref.at[rows, :],
            send_sem=w_send.at[index], recv_sem=w_recv.at[index], device_id=device, device_id_type=MESH,
        )
        copy.start()
        pending.append(copy.wait_send)

    for k in range(1, chips_x):
        send_piece(mine, k - 1, along(2 * k))
    send_piece(mine, chips_x - 1, sibling)
    tell(0, rounds[0])
    for load in loads[2:]:
        load.wait()
    ct_ref[...] = cot_ref[...].astype(F32).T.astype(BF16)
    bias_rows = lax.broadcasted_iota(jnp.int32, (8, OUTS), 0)
    bias_row = jnp.sum(jnp.where(bias_rows == bucket, bias_ref[...], 0.0), axis=0, keepdims=True)
    meta_ref[0] = jnp.where(bias_rows == 0, bias_row, count.astype(F32))

    for k in range(1, 4):
        to = pl.ds(pl.multiple_of(QUARTER * (q ^ k), QUARTER), QUARTER)
        send_block(meta_ref.at[0], meta_ref.at[k], m_send, m_recv, k)
        send_block(ct_ref.at[to, :], c4_ref.at[k], c_send, c_recv, k)
    quarter = pl.ds(pl.multiple_of(QUARTER * q, QUARTER), QUARTER)
    c4_ref[0] = ct_ref[quarter, :]

    for k in range(1, 4):
        wait_bytes(meta_ref.at[k], m_recv.at[k - 1])
    table = jnp.concatenate(
        [meta_ref[k, 0:1, :] for k in range(4)]
        + [gain_ref[...], shift_ref[...], jnp.zeros((122, OUTS), F32)],
        axis=0,
    )
    par_ref[...] = table.T
    params = par_ref[quarter, :]
    param_lane = lax.broadcasted_iota(jnp.int32, (QUARTER, OUTS), 1)

    def column(index):
        return jnp.sum(jnp.where(param_lane == index, params, 0.0), axis=1, keepdims=True)

    gain = column(4)
    shift = column(5)

    for k in range(1, chips_x):
        source = piece(chips_x - k)
        wait_bytes(wg_ref.at[source, :], w_recv.at[k - 1])
        send_piece(source, chips_x - 1 + k, sibling)
    hear(0, rounds[0])
    tell(1, rounds[1])
    for k in range(chips_x):
        wait_bytes(wg_ref.at[mine, :], w_recv.at[chips_x - 1 + k])
    for g in range(TILES):
        wt_ref[pl.ds(128 * g, 128), :] = wg_ref[:, pl.ds(128 * g, 128)].astype(F32).T.astype(BF16)

    zf, yf, xf = lane_fields()
    reach = {
        (axis, offset): inside(offset, field, cells).astype(F32)
        for axis, field, cells in (("z", zf, 4), ("y", yf, 8), ("x", xf, 8))
        for offset in (-1, 1)
    }

    def moved(value, axis, offset, step):
        if offset == 0:
            return value
        rolled = pltpu.roll(value, (-offset * step) % VOX, 1)
        return rolled * reach[axis, offset]

    def group_sum(value):
        grouped = value.reshape(QUARTER // 8, 8, VOX)
        total = jnp.sum(jnp.sum(grouped, axis=2, keepdims=True), axis=1, keepdims=True)
        return total


    lane = lax.broadcasted_iota(jnp.int32, (1, VOX), 1).astype(F32)

    def spread(total):
        return jnp.broadcast_to(total, (QUARTER // 8, 8, VOX)).reshape(QUARTER, VOX)

    def normalize(m, pre):
        cells = meta_ref[m][1:2, 0:1]
        mask = (lane < cells).astype(F32)
        inverse = (1.0 / (cells * 8.0)).reshape(1, 1, 1)
        mean = spread(group_sum(pre * mask) * inverse)
        centered = pre - mean
        variance = group_sum(centered * centered * mask) * inverse
        scale = spread(lax.rsqrt(variance + EPSILON))
        normed = centered * scale
        value = normed * gain + shift + column(m)
        sig = 1.0 / (1.0 + jnp.exp(-value))
        acts_ref[m] = (value * sig * mask).astype(BF16)
        d_normed = c4_ref[m].astype(F32) * mask * (sig * (1.0 + value * (1.0 - sig))) * gain
        mean_d = spread(group_sum(d_normed) * inverse)
        mean_dn = spread(group_sum(d_normed * normed) * inverse)
        grad = scale * (d_normed - mask * (mean_d + normed * mean_dn))
        return grad.astype(BF16).astype(F32)

    def crops_of(pair):
        xts, pre, sum_z, sum_y, grads = {}, {}, {}, {}, {}
        for m in pair:
            if m > 0:
                wait_bytes(x_ref.at[m], x_recv.at[m - 1])
                wait_bytes(c4_ref.at[m], c_recv.at[m - 1])
        for m in pair:
            xts[m] = x_ref[m].astype(F32).T.astype(BF16)
            xt_ref[m] = xts[m]
            pre[m] = jnp.zeros((QUARTER, VOX), F32)
        for g in range(TILES):
            for m in pair:
                product = jnp.dot(wt_ref[pl.ds(128 * g, 128), :], xts[m], preferred_element_type=F32)
                for j in range(4):
                    t = 4 * g + j
                    if t >= TAPS:
                        continue
                    a, b, e = t // 9 - 1, t // 3 % 3 - 1, t % 3 - 1
                    part = moved(product[32 * j : 32 * j + 32], "x", e, 1)
                    sum_y[m] = part if e == -1 else sum_y[m] + part
                    if e == 1:
                        part = moved(sum_y[m], "y", b, 8)
                        sum_z[m] = part if b == -1 else sum_z[m] + part
                        if b == 1:
                            pre[m] = pre[m] + moved(sum_z[m], "z", a, 64)
        for m in pair:
            grads[m] = normalize(m, pre[m])
        for a in range(-1, 2):
            grad_a = {m: moved(grads[m], "z", -a, 64) for m in pair}
            for b in range(-1, 2):
                grad_ab = {m: moved(grad_a[m], "y", -b, 8) for m in pair}
                for e in range(-1, 2):
                    t = 9 * (a + 1) + 3 * (b + 1) + e + 1
                    for m in pair:
                        g_ref[m, pl.ds(32 * t, 32), :] = moved(grad_ab[m], "x", -e, 1).astype(BF16)
        for m in pair:
            g_ref[m, pl.ds(32 * TAPS, 32), :] = jnp.zeros((32, VOX), BF16)

    crops_of((0, 1))
    crops_of((2, 3))
    hear(1, rounds[1])
    tell(2, rounds[2])

    for k in range(1, 4):
        copy = pltpu.make_async_remote_copy(
            src_ref=acts_ref.at[k], dst_ref=actr_ref.at[quarter, :],
            send_sem=a_send.at[k - 1], recv_sem=a_recv.at[k - 1],
            device_id=member(k), device_id_type=MESH,
        )
        copy.start()
        pending.append(copy.wait_send)
    actr_ref[quarter, :] = acts_ref[0]

    side_c = lax.rem(fs, 2)
    chip_x = fs // 2
    for index, (start, width) in enumerate(CHUNKS):
        lanes = pl.ds(start, width)
        total = jnp.zeros((chans, width), F32)
        for m in range(4):
            total = total + lax.dot_general(
                xt_ref[m], g_ref[m, lanes, :], (((1,), (1,)), ((), ())), preferred_element_type=F32
            )
        dwf_ref[:, :, :, lanes] = total.reshape(chips_x, 2, OWN, width)
        copy = pltpu.make_async_remote_copy(
            src_ref=dwf_ref.at[:, 1 - side_c, :, lanes], dst_ref=d0r_ref.at[:, :, lanes],
            send_sem=d0_send.at[index], recv_sem=d0_recv.at[index], device_id=sibling, device_id_type=MESH,
        )
        copy.start()
        pending.append(copy.wait_send)
    for index, (start, width) in enumerate(CHUNKS):
        lanes = pl.ds(start, width)
        wait_bytes(d0r_ref.at[:, :, lanes], d0_recv.at[index])
        total = dwf_ref[:, side_c, :, lanes] + d0r_ref[:, :, lanes]
        d0r_ref[:, :, lanes] = total
        d1s_ref[:, :, lanes] = total.astype(BF16)
        for k in range(1, chips_x):
            copy = pltpu.make_async_remote_copy(
                src_ref=d1s_ref.at[lax.rem(chip_x + k, chips_x), :, lanes], dst_ref=d1r_ref.at[k - 1, :, lanes],
                send_sem=d1_send.at[index, k - 1], recv_sem=d1_recv.at[index],
                device_id=along(2 * k), device_id_type=MESH,
            )
            copy.start()
            pending.append(copy.wait_send)
    hear(2, rounds[2])

    spacing = nzp // spots

    def owner(u):
        return u // per_row, u % per_row // per_dev * spacing

    for index, (start, width) in enumerate(CHUNKS):
        lanes = pl.ds(start, width)
        if chips_x > 1:
            wait_bytes(d1r_ref.at[:, :, lanes], d1_recv.at[index])
        total = d0r_ref[chip_x, :, lanes]
        for k in range(1, chips_x):
            total = total + d1r_ref[k - 1, :, lanes].astype(F32)
        for g in range(start // 128, (start + width) // 128):
            for h in range(2):
                u = 2 * g + h
                at = 128 * g - start
                s_ref[u] = total[16 * h : 16 * h + 16, at : at + 128]
                oy, oz = owner(u)
                away = jnp.logical_or(yp != oy, zp != oz)
                slot = lax.rem(yp - oy + nyp, nyp) * nzp + lax.rem(zp - oz + nzp, nzp) - 1
                copy = pltpu.make_async_remote_copy(
                    src_ref=s_ref.at[u],
                    dst_ref=r2_ref.at[u % per_dev, jnp.maximum(slot, 0)],
                    send_sem=d2_send.at[u], recv_sem=d2_recv.at[u % per_dev],
                    device_id=plane(2 * oy + qy, 2 * oz + qz), device_id_type=MESH,
                )
                pl.when(away)(copy.start)
                pending.append(functools.partial(pl.when(away), copy.wait_send))

    owns = lax.rem(zp, spacing) == 0
    my_spot = zp // spacing
    first = yp * per_row + my_spot * per_dev
    owns = jnp.logical_and(owns, first < REAL)
    own_units = f_ref.at[pl.ds(first, per_dev), qy, qz]

    def unit_copy(k):
        return pltpu.make_async_remote_copy(
            src_ref=own_units, dst_ref=own_units,
            send_sem=e1_send.at[k - 1], recv_sem=e1_recv.at[my_spot, qz],
            device_id=plane(y, lax.rem(z + k, nz)), device_id_type=MESH,
        )

    @pl.when(owns)
    def _():
        for i in range(per_dev):
            u = first + i

            @pl.when(u < REAL)
            def _():
                wait_bytes(r2_ref.at[i], d2_recv.at[i])
                total = s_ref[u]
                for k in range(nyp * nzp - 1):
                    total = total + r2_ref[i, k]
                f_ref[u, qy, qz] = total.astype(BF16)

            @pl.when(u >= REAL)
            def _():
                f_ref[u, qy, qz] = jnp.zeros((16, 128), BF16)

        for k in sorted(range(1, nz), key=lambda k: min(k, nz - k)):
            unit_copy(k).start()

    def sent():
        @pl.when(owns)
        def _():
            for k in range(1, nz):
                unit_copy(k).wait_send()

    pending.append(sent)

    for k in range(1, 4):
        theirs = pl.ds(pl.multiple_of(QUARTER * (q ^ k), QUARTER), QUARTER)
        wait_bytes(actr_ref.at[theirs, :], a_recv.at[k - 1])
    act_ref[...] = actr_ref[...].astype(F32).T.astype(BF16)


    def start_of(row, spot):
        return (row // 2) * per_row + spot * per_dev

    def row_units(row, spot):
        return f_ref.at[pl.ds(start_of(row, spot), per_dev), lax.rem(row, 2)]

    def row_copy(spot, k):
        return pltpu.make_async_remote_copy(
            src_ref=row_units(y, spot), dst_ref=row_units(y, spot),
            send_sem=e2_send.at[spot, k - 1], recv_sem=e2_recv.at[spot, k - 1],
            device_id=plane(lax.rem(y + k, ny), z), device_id_type=MESH,
        )

    far_first = sorted(range(1, ny), key=lambda k: -min(k, ny - k))

    def pass_on(spot):
        at = spot * spacing

        @pl.when(start_of(y, spot) < REAL)
        def _():
            for side in range(2):
                @pl.when(jnp.logical_not(jnp.logical_and(zp == at, qz == side)))
                def _():
                    units = f_ref.at[pl.ds(start_of(y, spot), per_dev), qy, side]
                    wait_bytes(units, e1_recv.at[spot, side])

            for k in far_first:
                row_copy(spot, k).start()

    def row_sent():
        for spot in range(spots):
            @pl.when(start_of(y, spot) < REAL)
            def _():
                for k in range(1, ny):
                    row_copy(spot, k).wait_send()

    pending.append(row_sent)
    nearest = (zp + spacing // 2) // spacing
    for step in (0, 1, spots - 1, 2)[:spots]:
        pass_on(lax.rem(nearest + step, spots))
    for k in range(1, ny):
        from_row = lax.rem(y + ny - k, ny)
        for spot in range(spots):
            @pl.when(start_of(from_row, spot) < REAL)
            def _():
                wait_bytes(row_units(from_row, spot), e2_recv.at[spot, k - 1])


    block16 = lax.broadcasted_iota(jnp.int32, (16, 128), 1) >> 5
    for g in range(TILES):
        for h in range(2):
            quarters = [f_ref[2 * g + h, p // 2, p % 2].astype(F32) for p in range(4)]
            for j in range(4):
                t = 4 * g + j
                if t >= TAPS:
                    continue
                line = jnp.zeros((16, 128), F32)
                for p in range(4):
                    turned = quarters[p] if p == j else pltpu.roll(quarters[p], (32 * (p - j)) % 128, 1)
                    line = jnp.where(block16 == p, turned, line)
                grad_ref[t, 16 * h : 16 * h + 16, :] = line
    for wait in pending:
        wait()

def body(geometry, crops, weight, bucket_bias, norm_gain, norm_shift, bucket_ids, valid_counts, cotangent):
    ny, nz, peers = geometry
    nyp, nzp = ny // 2, nz // 2
    per_row = UNITS // nyp
    spots = min(per_row, nzp, 4)
    per_dev = per_row // spots
    chans = OWN * peers
    others = max(1, peers - 1)
    smem = pl.BlockSpec(memory_space=pltpu.SMEM)
    vmem = pl.BlockSpec(memory_space=pltpu.VMEM)
    dma = pltpu.SemaphoreType.DMA
    def hold(x):
        return pltpu.with_memory_space_constraint(x, pltpu.HBM)

    activated, grad = pl.pallas_call(
        functools.partial(kernel, geometry),
        out_shape=(
            jax.ShapeDtypeStruct((VOX, OUTS), BF16),
            jax.ShapeDtypeStruct((TAPS, OWN, OUTS), F32),
        ),
        in_specs=[smem, smem] + [pl.BlockSpec(memory_space=pltpu.HBM)] * 6,
        out_specs=(vmem, vmem),
        scratch_shapes=[
            pltpu.VMEM((VOX, chans), BF16),
            pltpu.VMEM((TAPS, OWN, OUTS), BF16),
            pltpu.VMEM(bucket_bias.shape, F32),
            pltpu.VMEM((1, OUTS), F32),
            pltpu.VMEM((1, OUTS), F32),
            pltpu.VMEM((VOX, OUTS), BF16),
            dma((6,)),
            pltpu.VMEM((4, VOX, chans), BF16),
            pltpu.VMEM((4, chans, VOX), BF16),
            pltpu.VMEM((chans, COLS), BF16),
            pltpu.VMEM((COLS, chans), BF16),
            pltpu.VMEM((OUTS, VOX), BF16),
            pltpu.VMEM((4, QUARTER, VOX), BF16),
            pltpu.VMEM((4, 8, OUTS), F32),
            pltpu.VMEM((OUTS, OUTS), F32),
            pltpu.VMEM((4, COLS, VOX), BF16),
            pltpu.VMEM((peers // 2, 2, OWN, COLS), F32),
            pltpu.VMEM((peers // 2, OWN, COLS), F32),
            pltpu.VMEM((peers // 2, OWN, COLS), BF16),
            pltpu.VMEM((max(1, peers // 2 - 1), OWN, COLS), BF16),
            pltpu.VMEM((REAL, 16, 128), F32),
            pltpu.VMEM((per_dev, max(1, nyp * nzp - 1), 16, 128), F32),
            pltpu.VMEM((UNITS, 2, 2, 16, 128), BF16),
            pltpu.VMEM((4, QUARTER, VOX), BF16),
            pltpu.VMEM((OUTS, VOX), BF16),
            pltpu.SemaphoreType.REGULAR((3,)),
            dma((others,)), dma((others,)),
            dma((3,)), dma((3,)),
            dma((3,)), dma((3,)),
            dma((3,)), dma((3,)),
            dma((3,)), dma((3,)),
            dma((len(CHUNKS),)), dma((len(CHUNKS),)),
            dma((len(CHUNKS), others)), dma((len(CHUNKS),)),
            dma((REAL,)), dma((per_dev,)),
            dma((nz - 1,)), dma((spots, 2)),
            dma((spots, ny - 1)), dma((spots, ny - 1)),
        ],
        compiler_params=pltpu.CompilerParams(
            collective_id=0, has_side_effects=True, vmem_limit_bytes=40 * 1024 * 1024
        ),
    )(
        valid_counts, bucket_ids,
        hold(crops.reshape(VOX, chans)), hold(weight.transpose(1, 0, 2)), hold(bucket_bias),
        hold(norm_gain.reshape(1, OUTS)), hold(norm_shift.reshape(1, OUTS)), hold(cotangent.reshape(VOX, OUTS)),
    )
    return activated[None], grad.transpose(1, 0, 2)


def solution(mesh):
    chips = mesh.shape["dp"]
    ny = 8 if chips == 128 else 2
    geometry = (ny, chips // ny, mesh.shape["fsdp"])
    return jax.shard_map(
        functools.partial(body, geometry),
        mesh=mesh,
        in_specs=(
            P(("dp", "fsdp"), None, None, None, None),
            P("fsdp", None, None),
            P(),
            P(),
            P(),
            P(("dp", "fsdp")),
            P(("dp", "fsdp")),
            P(("dp", "fsdp"), None, None),
        ),
        out_specs=(P(("dp", "fsdp"), None, None), P("fsdp", None, None)),
        check_vma=False,
    )
```

time: 78.9 us -> 69.5 us (0.88)
  the two profiles are of different devices: /device:TPU:1 before, /device:TPU:8 now
where the time goes in v2:
time: 69.5 us; the launch traced here: 69.3 us
  Pallas kernels  66 us (95%)
  between operations  1.93 us (3%)
  local copies, waits for them, and re-layouts  1.39 us (2%)
    pallas_call x1, Pallas kernels, body(): pl.pallas_call(functools.partial(kernel, geometry), out_shape=(jax.ShapeD...  66 us
    unnamed x2, local copies, waits for them, and re-layouts  1.39 us

profile of v2, /device:TPU:8, one launch (start us, length us, event | category | flops | bytes accessed | tf_op | source)
XLA Modules:
  0.0 69.3 jit_solution(13646278887607736907)
XLA Ops:
  1.9 66.0 %shard_map.95 = (bf16[256,128]{1,0:T(8,128)(2,1)S(1)}, f32[27,32,128]{2,1,0:T(8,128)S(1)}) custom-call(s32[1]{0:T(128)S(6)} %copy.13.count_ref, s32[1]{0:T(128)S(6)} %copy.12.bucket_ref, bf16[256,256]{1,0:T(8,128)(2,1)} %bitcast.10, bf16[27,32,128]{2,1,0:T(8,128)(2,1)} %bitcast.9, f32[8,128]{1,0:T(8,128)} %bias_hbm.1, f32[1,128]{1,0:T(1,128)} %bitcast.12, ...), custom_call_target="tpu_custom_call" | custom-call | tf_op jit(solution)/shard_map/pallas_call | solution.py:493
  67.9 0.6 copy.14
  68.5 0.8 %copy.15 = f32[32,27,128]{2,0,1:T(8,128)} copy(f32[32,27,128]{2,0,1:T(8,128)S(1)} %bitcast.7) | data formatting | bytes 884736

commit v3 on v2

--- a/solution.py
+++ b/solution.py
@@ -91,8 +91,12 @@
         greet(member(k))
     greeted = peers - 1 + 3
 
-    beside = sorted({(a % nyp, b % nzp) for a in (-1, 0, 1) for b in (-1, 0, 1)} - {(0, 0)})
-    beyond = sorted({2 % nzp, -2 % nzp} - {0})
+    def offsets(*pairs):
+        return sorted({(a % nyp, b % nzp) for a, b in pairs} - {(0, 0)})
+
+    beside = offsets((0, 1), (0, -1), (1, 0), (-1, 0))
+    second = offsets((0, 2), (0, -2), (2, 0), (1, 1), (1, -1), (-1, 1), (-1, -1))
+    along_z = offsets((0, 2), (0, -2))
 
     def block(a, b):
         return plane(2 * lax.rem(yp + a, nyp) + qy, 2 * lax.rem(zp + b, nzp) + qz)
@@ -111,7 +115,8 @@
 
     rounds = (
         [block(a, b) for a, b in beside],
-        [block(0, b) for b in beyond],
+        [block(a, b) for a, b in second],
+        [block(a, b) for a, b in along_z],
         [member(k) for k in range(1, 4)],
     )
 
@@ -121,20 +126,6 @@
     row_mask = (rows < count).astype(F32)
     loads[0].wait()
     x_ref[0] = (crop_ref[...].astype(F32) * row_mask).astype(BF16)
-
-    pl.semaphore_wait(barrier, greeted)
-    pending = []
-
-    def send_block(src, dst, send, recv, k):
-        copy = pltpu.make_async_remote_copy(
-            src_ref=src, dst_ref=dst, send_sem=send.at[k - 1], recv_sem=recv.at[k - 1],
-            device_id=member(k), device_id_type=MESH,
-        )
-        copy.start()
-        pending.append(copy.wait_send)
-
-    for k in (3, 1, 2):
-        send_block(x_ref.at[0], x_ref.at[k], x_send, x_recv, k)
 
     lane_block = lax.broadcasted_iota(jnp.int32, (OWN, 128), 1) >> 5
     mine = pl.ds(pl.multiple_of(OWN * fs, OWN), OWN)
@@ -148,6 +139,23 @@
                 tile = jnp.where(lane_block == j, tap, tile)
         wg_ref[mine, pl.ds(128 * g, 128)] = tile.astype(BF16)
 
+    for load in loads[2:]:
+        load.wait()
+    ct_ref[...] = cot_ref[...].astype(F32).T.astype(BF16)
+    bias_rows = lax.broadcasted_iota(jnp.int32, (8, OUTS), 0)
+    bias_row = jnp.sum(jnp.where(bias_rows == bucket, bias_ref[...], 0.0), axis=0, keepdims=True)
+    meta_ref[0] = jnp.where(bias_rows == 0, bias_row, count.astype(F32))
+
+    pl.semaphore_wait(barrier, greeted)
+    pending = []
+
+    def send_block(src, dst, send, recv, k):
+        copy = pltpu.make_async_remote_copy(
+            src_ref=src, dst_ref=dst, send_sem=send.at[k - 1], recv_sem=recv.at[k - 1],
+            device_id=member(k), device_id_type=MESH,
+        )
+        copy.start()
+        pending.append(copy.wait_send)
 
     chips_x = peers // 2
     sibling = (dp, fs + 1 - 2 * lax.rem(fs, 2))
@@ -166,18 +174,15 @@
     for k in range(1, chips_x):
         send_piece(mine, k - 1, along(2 * k))
     send_piece(mine, chips_x - 1, sibling)
-    tell(0, rounds[0])
-    for load in loads[2:]:
-        load.wait()
-    ct_ref[...] = cot_ref[...].astype(F32).T.astype(BF16)
-    bias_rows = lax.broadcasted_iota(jnp.int32, (8, OUTS), 0)
-    bias_row = jnp.sum(jnp.where(bias_rows == bucket, bias_ref[...], 0.0), axis=0, keepdims=True)
-    meta_ref[0] = jnp.where(bias_rows == 0, bias_row, count.astype(F32))
+    for k in range(1, 4):
+        send_block(meta_ref.at[0], meta_ref.at[k], m_send, m_recv, k)
+    for k in (3, 1, 2):
+        send_block(x_ref.at[0], x_ref.at[k], x_send, x_recv, k)
 
     for k in range(1, 4):
         to = pl.ds(pl.multiple_of(QUARTER * (q ^ k), QUARTER), QUARTER)
-        send_block(meta_ref.at[0], meta_ref.at[k], m_send, m_recv, k)
         send_block(ct_ref.at[to, :], c4_ref.at[k], c_send, c_recv, k)
+    tell(0, rounds[0])
     quarter = pl.ds(pl.multiple_of(QUARTER * q, QUARTER), QUARTER)
     c4_ref[0] = ct_ref[quarter, :]
 
@@ -189,6 +194,8 @@
         axis=0,
     )
     par_ref[...] = table.T
+    hear(0, rounds[0])
+    tell(1, rounds[1])
     params = par_ref[quarter, :]
     param_lane = lax.broadcasted_iota(jnp.int32, (QUARTER, OUTS), 1)
 
@@ -202,8 +209,6 @@
         source = piece(chips_x - k)
         wait_bytes(wg_ref.at[source, :], w_recv.at[k - 1])
         send_piece(source, chips_x - 1 + k, sibling)
-    hear(0, rounds[0])
-    tell(1, rounds[1])
     for k in range(chips_x):
         wait_bytes(wg_ref.at[mine, :], w_recv.at[chips_x - 1 + k])
     for g in range(TILES):
@@ -251,12 +256,11 @@
         grad = scale * (d_normed - mask * (mean_d + normed * mean_dn))
         return grad.astype(BF16).astype(F32)
 
-    def crops_of(pair):
+    def crops_of(pair, between=None):
         xts, pre, sum_z, sum_y, grads = {}, {}, {}, {}, {}
         for m in pair:
             if m > 0:
                 wait_bytes(x_ref.at[m], x_recv.at[m - 1])
-                wait_bytes(c4_ref.at[m], c_recv.at[m - 1])
         for m in pair:
             xts[m] = x_ref[m].astype(F32).T.astype(BF16)
             xt_ref[m] = xts[m]
@@ -276,6 +280,11 @@
                         sum_z[m] = part if b == -1 else sum_z[m] + part
                         if b == 1:
                             pre[m] = pre[m] + moved(sum_z[m], "z", a, 64)
+        if between is not None:
+            between()
+        for m in pair:
+            if m > 0:
+                wait_bytes(c4_ref.at[m], c_recv.at[m - 1])
         for m in pair:
             grads[m] = normalize(m, pre[m])
         for a in range(-1, 2):
@@ -289,11 +298,24 @@
         for m in pair:
             g_ref[m, pl.ds(32 * TAPS, 32), :] = jnp.zeros((32, VOX), BF16)
 
-    crops_of((0, 1))
+    def gradient(pair, lanes, width):
+        total = None
+        for m in pair:
+            term = lax.dot_general(
+                xt_ref[m], g_ref[m, lanes, :], (((1,), (1,)), ((), ())), preferred_element_type=F32
+            )
+            total = term if total is None else total + term
+        return total.reshape(chips_x, 2, OWN, width)
+
+    def second_round():
+        hear(1, rounds[1])
+        tell(2, rounds[2])
+
+    crops_of((0, 1), second_round)
+    for start, width in CHUNKS:
+        lanes = pl.ds(start, width)
+        dwf_ref[:, :, :, lanes] = gradient((0, 1), lanes, width)
     crops_of((2, 3))
-    hear(1, rounds[1])
-    tell(2, rounds[2])
-
     for k in range(1, 4):
         copy = pltpu.make_async_remote_copy(
             src_ref=acts_ref.at[k], dst_ref=actr_ref.at[quarter, :],
@@ -308,25 +330,22 @@
     chip_x = fs // 2
     for index, (start, width) in enumerate(CHUNKS):
         lanes = pl.ds(start, width)
-        total = jnp.zeros((chans, width), F32)
-        for m in range(4):
-            total = total + lax.dot_general(
-                xt_ref[m], g_ref[m, lanes, :], (((1,), (1,)), ((), ())), preferred_element_type=F32
-            )
-        dwf_ref[:, :, :, lanes] = total.reshape(chips_x, 2, OWN, width)
+        dwf_ref[:, :, :, lanes] += gradient((2, 3), lanes, width)
         copy = pltpu.make_async_remote_copy(
             src_ref=dwf_ref.at[:, 1 - side_c, :, lanes], dst_ref=d0r_ref.at[:, :, lanes],
             send_sem=d0_send.at[index], recv_sem=d0_recv.at[index], device_id=sibling, device_id_type=MESH,
         )
         copy.start()
         pending.append(copy.wait_send)
+    hear(2, rounds[2])
+    tell(3, rounds[3])
     for index, (start, width) in enumerate(CHUNKS):
         lanes = pl.ds(start, width)
         wait_bytes(d0r_ref.at[:, :, lanes], d0_recv.at[index])
         total = dwf_ref[:, side_c, :, lanes] + d0r_ref[:, :, lanes]
         d0r_ref[:, :, lanes] = total
         d1s_ref[:, :, lanes] = total.astype(BF16)
-        for k in range(1, chips_x):
+        for k in sorted(range(1, chips_x), key=lambda k: -min(k, chips_x - k)):
             copy = pltpu.make_async_remote_copy(
                 src_ref=d1s_ref.at[lax.rem(chip_x + k, chips_x), :, lanes], dst_ref=d1r_ref.at[k - 1, :, lanes],
                 send_sem=d1_send.at[index, k - 1], recv_sem=d1_recv.at[index],
@@ -334,12 +353,12 @@
             )
             copy.start()
             pending.append(copy.wait_send)
-    hear(2, rounds[2])
+    hear(3, rounds[3])
 
     spacing = nzp // spots
 
     def owner(u):
-        return u // per_row, u % per_row // per_dev * spacing
+        return u // per_row, u % per_row // per_dev * spacing + spacing - 1
 
     for index, (start, width) in enumerate(CHUNKS):
         lanes = pl.ds(start, width)
@@ -365,17 +384,17 @@
                 pl.when(away)(copy.start)
                 pending.append(functools.partial(pl.when(away), copy.wait_send))
 
-    owns = lax.rem(zp, spacing) == 0
+    owns = lax.rem(zp, spacing) == spacing - 1
     my_spot = zp // spacing
     first = yp * per_row + my_spot * per_dev
     owns = jnp.logical_and(owns, first < REAL)
     own_units = f_ref.at[pl.ds(first, per_dev), qy, qz]
 
-    def unit_copy(k):
+    def unit_copy(target):
         return pltpu.make_async_remote_copy(
             src_ref=own_units, dst_ref=own_units,
-            send_sem=e1_send.at[k - 1], recv_sem=e1_recv.at[my_spot, qz],
-            device_id=plane(y, lax.rem(z + k, nz)), device_id_type=MESH,
+            send_sem=e1_send.at[target], recv_sem=e1_recv.at[my_spot, qz],
+            device_id=plane(y, target), device_id_type=MESH,
         )
 
     @pl.when(owns)
@@ -395,14 +414,14 @@
             def _():
                 f_ref[u, qy, qz] = jnp.zeros((16, 128), BF16)
 
-        for k in sorted(range(1, nz), key=lambda k: min(k, nz - k)):
-            unit_copy(k).start()
+        for target in range(nz):
+            pl.when(z != target)(unit_copy(target).start)
 
     def sent():
         @pl.when(owns)
         def _():
-            for k in range(1, nz):
-                unit_copy(k).wait_send()
+            for target in range(nz):
+                pl.when(z != target)(unit_copy(target).wait_send)
 
     pending.append(sent)
 
@@ -428,7 +447,7 @@
     far_first = sorted(range(1, ny), key=lambda k: -min(k, ny - k))
 
     def pass_on(spot):
-        at = spot * spacing
+        at = spot * spacing + spacing - 1
 
         @pl.when(start_of(y, spot) < REAL)
         def _():
@@ -449,8 +468,8 @@
                     row_copy(spot, k).wait_send()
 
     pending.append(row_sent)
-    nearest = (zp + spacing // 2) // spacing
-    for step in (0, 1, spots - 1, 2)[:spots]:
+    nearest = zp // spacing
+    for step in {4: (0, 3, 1, 2), 2: (0, 1), 1: (0,)}[spots]:
         pass_on(lax.rem(nearest + step, spots))
     for k in range(1, ny):
         from_row = lax.rem(y + ny - k, ny)
@@ -524,7 +543,7 @@
             pltpu.VMEM((UNITS, 2, 2, 16, 128), BF16),
             pltpu.VMEM((4, QUARTER, VOX), BF16),
             pltpu.VMEM((OUTS, VOX), BF16),
-            pltpu.SemaphoreType.REGULAR((3,)),
+            pltpu.SemaphoreType.REGULAR((4,)),
             dma((others,)), dma((others,)),
             dma((3,)), dma((3,)),
             dma((3,)), dma((3,)),
@@ -533,7 +552,7 @@
             dma((len(CHUNKS),)), dma((len(CHUNKS),)),
             dma((len(CHUNKS), others)), dma((len(CHUNKS),)),
             dma((REAL,)), dma((per_dev,)),
-            dma((nz - 1,)), dma((spots, 2)),
+            dma((nz,)), dma((spots, 2)),
             dma((spots, ny - 1)), dma((spots, ny - 1)),
         ],
         compiler_params=pltpu.CompilerParams(

time: 69.5 us -> 66.7 us (0.960)
  the two profiles are of different devices: /device:TPU:8 before, /device:TPU:1 now
where the time goes in v3:
time: 66.7 us; the launch traced here: 66.5 us
  Pallas kernels  63.2 us (95%)
  between operations  1.93 us (3%)
  local copies, waits for them, and re-layouts  1.39 us (2%)
    pallas_call x1, Pallas kernels, body(): pl.pallas_call(functools.partial(kernel, geometry), out_shape=(jax.ShapeD...  63.2 us
    unnamed x2, local copies, waits for them, and re-layouts  1.39 us

profile of v3, /device:TPU:1, one launch (start us, length us, event | category | flops | bytes accessed | tf_op | source)
XLA Modules:
  0.0 66.5 jit_solution(5628310547718754151)
XLA Ops:
  1.9 63.2 %shard_map.95 = (bf16[256,128]{1,0:T(8,128)(2,1)S(1)}, f32[27,32,128]{2,1,0:T(8,128)S(1)}) custom-call(s32[1]{0:T(128)S(6)} %copy.13.count_ref, s32[1]{0:T(128)S(6)} %copy.12.bucket_ref, bf16[256,256]{1,0:T(8,128)(2,1)} %bitcast.10, bf16[27,32,128]{2,1,0:T(8,128)(2,1)} %bitcast.9, f32[8,128]{1,0:T(8,128)} %bias_hbm.1, f32[1,128]{1,0:T(1,128)} %bitcast.12, ...), custom_call_target="tpu_custom_call" | custom-call | tf_op jit(solution)/shard_map/pallas_call | solution.py:512
  65.1 0.6 copy.14
  65.7 0.8 %copy.15 = f32[32,27,128]{2,0,1:T(8,128)} copy(f32[32,27,128]{2,0,1:T(8,128)S(1)} %bitcast.7) | data formatting | bytes 884736

commit v4 on v3

--- a/solution.py
+++ b/solution.py
@@ -21,6 +21,7 @@
 COLS = TILES * 128
 UNITS = 16
 REAL = 2 * TILES
+SPOTS = {8: (7, 0, 1, 5)}
 CHUNKS = ((0, 256), (256, 256), (512, 256), (768, 128))
 
 
@@ -51,7 +52,8 @@
     ny, nz, peers = geometry
     nyp, nzp = ny // 2, nz // 2
     per_row = UNITS // nyp
-    spots = min(per_row, nzp, 4)
+    places = SPOTS.get(nzp, tuple(range(min(per_row, nzp, 4))))
+    spots = len(places)
     per_dev = per_row // spots
     chans = OWN * peers
 
@@ -176,7 +178,7 @@
     send_piece(mine, chips_x - 1, sibling)
     for k in range(1, 4):
         send_block(meta_ref.at[0], meta_ref.at[k], m_send, m_recv, k)
-    for k in (3, 1, 2):
+    for k in (1, 3, 2):
         send_block(x_ref.at[0], x_ref.at[k], x_send, x_recv, k)
 
     for k in range(1, 4):
@@ -344,7 +346,7 @@
         wait_bytes(d0r_ref.at[:, :, lanes], d0_recv.at[index])
         total = dwf_ref[:, side_c, :, lanes] + d0r_ref[:, :, lanes]
         d0r_ref[:, :, lanes] = total
-        d1s_ref[:, :, lanes] = total.astype(BF16)
+        d1s_ref[:, :, lanes] = total
         for k in sorted(range(1, chips_x), key=lambda k: -min(k, chips_x - k)):
             copy = pltpu.make_async_remote_copy(
                 src_ref=d1s_ref.at[lax.rem(chip_x + k, chips_x), :, lanes], dst_ref=d1r_ref.at[k - 1, :, lanes],
@@ -355,10 +357,8 @@
             pending.append(copy.wait_send)
     hear(3, rounds[3])
 
-    spacing = nzp // spots
-
     def owner(u):
-        return u // per_row, u % per_row // per_dev * spacing + spacing - 1
+        return u // per_row, places[u % per_row // per_dev]
 
     for index, (start, width) in enumerate(CHUNKS):
         lanes = pl.ds(start, width)
@@ -371,7 +371,7 @@
             for h in range(2):
                 u = 2 * g + h
                 at = 128 * g - start
-                s_ref[u] = total[16 * h : 16 * h + 16, at : at + 128]
+                s_ref[u] = total[16 * h : 16 * h + 16, at : at + 128].astype(BF16)
                 oy, oz = owner(u)
                 away = jnp.logical_or(yp != oy, zp != oz)
                 slot = lax.rem(yp - oy + nyp, nyp) * nzp + lax.rem(zp - oz + nzp, nzp) - 1
@@ -384,8 +384,8 @@
                 pl.when(away)(copy.start)
                 pending.append(functools.partial(pl.when(away), copy.wait_send))
 
-    owns = lax.rem(zp, spacing) == spacing - 1
-    my_spot = zp // spacing
+    owns = functools.reduce(jnp.logical_or, [zp == place for place in places])
+    my_spot = sum(jnp.where(zp == place, spot, 0) for spot, place in enumerate(places))
     first = yp * per_row + my_spot * per_dev
     owns = jnp.logical_and(owns, first < REAL)
     own_units = f_ref.at[pl.ds(first, per_dev), qy, qz]
@@ -405,9 +405,9 @@
             @pl.when(u < REAL)
             def _():
                 wait_bytes(r2_ref.at[i], d2_recv.at[i])
-                total = s_ref[u]
+                total = s_ref[u].astype(F32)
                 for k in range(nyp * nzp - 1):
-                    total = total + r2_ref[i, k]
+                    total = total + r2_ref[i, k].astype(F32)
                 f_ref[u, qy, qz] = total.astype(BF16)
 
             @pl.when(u >= REAL)
@@ -446,9 +446,7 @@
 
     far_first = sorted(range(1, ny), key=lambda k: -min(k, ny - k))
 
-    def pass_on(spot):
-        at = spot * spacing + spacing - 1
-
+    def pass_on(spot, at):
         @pl.when(start_of(y, spot) < REAL)
         def _():
             for side in range(2):
@@ -468,9 +466,8 @@
                     row_copy(spot, k).wait_send()
 
     pending.append(row_sent)
-    nearest = zp // spacing
-    for step in {4: (0, 3, 1, 2), 2: (0, 1), 1: (0,)}[spots]:
-        pass_on(lax.rem(nearest + step, spots))
+    for spot, place in enumerate(places):
+        pass_on(spot, place)
     for k in range(1, ny):
         from_row = lax.rem(y + ny - k, ny)
         for spot in range(spots):
@@ -499,7 +496,8 @@
     ny, nz, peers = geometry
     nyp, nzp = ny // 2, nz // 2
     per_row = UNITS // nyp
-    spots = min(per_row, nzp, 4)
+    places = SPOTS.get(nzp, tuple(range(min(per_row, nzp, 4))))
+    spots = len(places)
     per_dev = per_row // spots
     chans = OWN * peers
     others = max(1, peers - 1)
@@ -536,10 +534,10 @@
             pltpu.VMEM((4, COLS, VOX), BF16),
             pltpu.VMEM((peers // 2, 2, OWN, COLS), F32),
             pltpu.VMEM((peers // 2, OWN, COLS), F32),
-            pltpu.VMEM((peers // 2, OWN, COLS), BF16),
-            pltpu.VMEM((max(1, peers // 2 - 1), OWN, COLS), BF16),
-            pltpu.VMEM((REAL, 16, 128), F32),
-            pltpu.VMEM((per_dev, max(1, nyp * nzp - 1), 16, 128), F32),
+            pltpu.VMEM((peers // 2, OWN, COLS), F32),
+            pltpu.VMEM((max(1, peers // 2 - 1), OWN, COLS), F32),
+            pltpu.VMEM((REAL, 16, 128), BF16),
+            pltpu.VMEM((per_dev, max(1, nyp * nzp - 1), 16, 128), BF16),
             pltpu.VMEM((UNITS, 2, 2, 16, 128), BF16),
             pltpu.VMEM((4, QUARTER, VOX), BF16),
             pltpu.VMEM((OUTS, VOX), BF16),

time: 66.7 us -> 64 us (0.960)
  Pallas kernels: 63.2 us -> 60.5 us
    pallas_call x1, Pallas kernels: 63.2 us -> 60.5 us  [body(): pl.pallas_call(functools.partial(kernel, geometry), out_shape=(jax.ShapeD...]
where the time goes in v4:
time: 64 us; the launch traced here: 63.8 us
  Pallas kernels  60.5 us (95%)
  between operations  1.93 us (3%)
  local copies, waits for them, and re-layouts  1.39 us (2%)
    pallas_call x1, Pallas kernels, body(): pl.pallas_call(functools.partial(kernel, geometry), out_shape=(jax.ShapeD...  60.5 us
    unnamed x2, local copies, waits for them, and re-layouts  1.39 us

profile of v4, /device:TPU:1, one launch (start us, length us, event | category | flops | bytes accessed | tf_op | source)
XLA Modules:
  0.0 63.8 jit_solution(2942016550208163459)
XLA Ops:
  1.9 60.5 %shard_map.95 = (bf16[256,128]{1,0:T(8,128)(2,1)S(1)}, f32[27,32,128]{2,1,0:T(8,128)S(1)}) custom-call(s32[1]{0:T(128)S(6)} %copy.13.count_ref, s32[1]{0:T(128)S(6)} %copy.12.bucket_ref, bf16[256,256]{1,0:T(8,128)(2,1)} %bitcast.10, bf16[27,32,128]{2,1,0:T(8,128)(2,1)} %bitcast.9, f32[8,128]{1,0:T(8,128)} %bias_hbm.1, f32[1,128]{1,0:T(1,128)} %bitcast.12, ...), custom_call_target="tpu_custom_call" | custom-call | tf_op jit(solution)/shard_map/pallas_call | solution.py:510
  62.4 0.6 copy.14
  63.0 0.8 %copy.15 = f32[32,27,128]{2,0,1:T(8,128)} copy(f32[32,27,128]{2,0,1:T(8,128)S(1)} %bitcast.7) | data formatting | bytes 884736

commit v5 on v4

--- a/solution.py
+++ b/solution.py
@@ -21,7 +21,7 @@
 COLS = TILES * 128
 UNITS = 16
 REAL = 2 * TILES
-SPOTS = {8: (7, 0, 1, 5)}
+SPOTS = {8: (7, 0, 6, 1)}
 CHUNKS = ((0, 256), (256, 256), (512, 256), (768, 128))
 
 

time: 64 us -> 63.9 us (level)
  no operation moved by 1% of the time
where the time goes in v5:
time: 63.9 us; the launch traced here: 63.7 us
  Pallas kernels  60.4 us (95%)
  between operations  1.93 us (3%)
  local copies, waits for them, and re-layouts  1.39 us (2%)
    pallas_call x1, Pallas kernels, body(): pl.pallas_call(functools.partial(kernel, geometry), out_shape=(jax.ShapeD...  60.4 us
    unnamed x2, local copies, waits for them, and re-layouts  1.39 us

profile of v5, /device:TPU:1, one launch (start us, length us, event | category | flops | bytes accessed | tf_op | source)
XLA Modules:
  0.0 63.7 jit_solution(17632932041540789437)
XLA Ops:
  1.9 60.4 %shard_map.95 = (bf16[256,128]{1,0:T(8,128)(2,1)S(1)}, f32[27,32,128]{2,1,0:T(8,128)S(1)}) custom-call(s32[1]{0:T(128)S(6)} %copy.13.count_ref, s32[1]{0:T(128)S(6)} %copy.12.bucket_ref, bf16[256,256]{1,0:T(8,128)(2,1)} %bitcast.10, bf16[27,32,128]{2,1,0:T(8,128)(2,1)} %bitcast.9, f32[8,128]{1,0:T(8,128)} %bias_hbm.1, f32[1,128]{1,0:T(1,128)} %bitcast.12, ...), custom_call_target="tpu_custom_call" | custom-call | tf_op jit(solution)/shard_map/pallas_call | solution.py:510
  62.3 0.6 copy.14
  62.9 0.8 %copy.15 = f32[32,27,128]{2,0,1:T(8,128)} copy(f32[32,27,128]{2,0,1:T(8,128)S(1)} %bitcast.7) | data formatting | bytes 884736
